TPU v7x, 32 devices: a whole 2x2x4 slice. The times are simulated.
32 devices in a mesh: ctx: 8 (over y, x, core), head: 4 (over z).
Axes of the slice: x: 2, y: 2, z: 4, core: 2. Of those that a mesh axis runs over, the one named last changes fastest.
Arguments:
- queries: bfloat16 [8192, 512], P('ctx', 'head'), may hold values from -6 to 6
- keys: bfloat16 [8192, 512], P('ctx', 'head'), may hold values from -6 to 6
- values: bfloat16 [8192, 4096], P('ctx', 'head'), may hold values from -6 to 6
- conv_weight: float32 [3, 4096], P(None, 'head'), may hold values from -3 to 3
- gain: float32 [4096], P('head'), may hold values from 0.5 to 1.5
- cotangent: bfloat16 [8192, 4096], P('ctx', 'head'), may hold values from -6 to 6
Outputs:
- normed: bfloat16 [8192, 4096], P('ctx', 'head')
- grad_q: bfloat16 [8192, 512], P('ctx', 'head')
- grad_k: bfloat16 [8192, 512], P('ctx', 'head')
- grad_v: bfloat16 [8192, 4096], P('ctx', 'head')
All inputs are finite; a program needn't handle non-finite values.
Results may differ from a plain program's by a relative error of at most 0.0068.
Values may be sent and summed in bfloat16 or wider, within the bound.
A program may use at most 192 MiB of HBM per device.

v0:
```python
import functools
import math

import jax
import jax.numpy as jnp
from jax import lax
from jax.experimental import pallas as pl
from jax.experimental.pallas import tpu as pltpu
from jax.sharding import PartitionSpec as P

FEAT = 16
CONV = 3
ROWS = 160
TILE = 256
S = 0.25 / math.sqrt(2.0)
EPS = 1e-06
F32 = jnp.float32
BF = jnp.bfloat16
LIMIT = 56 * 1024 * 1024


def dot(a, b):
    return jnp.dot(a, b, preferred_element_type=F32)


def dot_nt(a, b):
    return lax.dot_general(a, b, (((1,), (1,)), ((), ())), preferred_element_type=F32)


def dot_tn(a, b):
    return lax.dot_general(a, b, (((0,), (0,)), ((), ())), preferred_element_type=F32)


def turned(x, d):
    return pltpu.roll(x, FEAT - d, 0)


def phi(x, pair):
    parts = [x * 0.5, (x * x) * S]
    for d in range(1, 8):
        parts.append((x * turned(x, d)) * (pair * S))
    parts.append((x[:8] * x[8:]) * (pair * S))
    row = lax.broadcasted_iota(jnp.int32, (8, x.shape[1]), 0)
    parts.append(jnp.where(row == 0, 1.0, 0.0).astype(F32))
    return jnp.concatenate(parts, axis=0).astype(BF)


def phi_grad(g, x):
    total = g[16:32] * x
    for d in range(1, 8):
        part = g[16 + 16 * d : 32 + 16 * d]
        total = total + part * turned(x, d) + pltpu.roll(part * x, d, 0)
    last = g[144:152]
    total = total + jnp.concatenate([last * x[8:], last * x[:8]], axis=0)
    return g[:16] * 0.5 + (2.0 * S) * total


def lanes(rows):
    return lax.broadcasted_iota(jnp.int32, (rows, 128), 1)


def with_ones(conv):
    ones = jnp.where(lanes(conv.shape[0]) < 2, 1.0, 0.0).astype(BF)
    return jnp.concatenate([conv, ones], axis=1)


def with_split(wide, column, order):
    high = column.astype(BF).astype(F32)
    low = column - high
    lane = lanes(wide.shape[0])
    right = jnp.zeros(lane.shape, F32)
    for at, kind in enumerate(order):
        right = jnp.where(lane == at, high if kind == "h" else low, right)
    return jnp.concatenate([wide.astype(BF), right.astype(BF)], axis=1)


def state_kernel(values_ref, prev_ref, taps_ref, kt_ref, conv_ref, state_ref):
    v = values_ref[...].astype(F32)
    row = lax.broadcasted_iota(jnp.int32, v.shape, 0)
    one = jnp.where(row == 0, prev_ref[1:2], pltpu.roll(v, 1, 0))
    two = jnp.where(
        row == 0, prev_ref[0:1], jnp.where(row == 1, prev_ref[1:2], pltpu.roll(v, 2, 0))
    )
    conv = (taps_ref[0:1] * v + taps_ref[1:2] * one + taps_ref[2:3] * two).astype(BF)
    conv_ref[...] = conv
    total = dot(phi(kt_ref[...].astype(F32), 1.0), with_ones(conv))
    state_ref[0] = with_split(total[:, :128], total[:, 128:129], "hl")


def head_rows(ref, h):
    row = lax.broadcasted_iota(jnp.int32, (ref.shape[0], 1), 0)
    return (ref[...].astype(F32) * jnp.where(row // FEAT == h, 1.0, 0.0)).astype(BF)


def head_lanes(ref, h):
    lane = lax.broadcasted_iota(jnp.int32, (1, ref.shape[1]), 1)
    return (ref[...].astype(F32) * jnp.where(lane // FEAT == h, 1.0, 0.0)).astype(BF)


def forward_kernel(
    index_ref, all_ref, q_ref, kt_ref, qth_ref, conv_ref, cot_ref, gain_ref,
    att_ref, den_ref, stat_ref, prior_ref, sums,
):
    h = pl.program_id(0)
    me = index_ref[0]
    total = jnp.zeros((ROWS, 256), F32)
    for j in range(all_ref.shape[0]):
        total = total + jnp.where(j < me, all_ref[j, 0].astype(F32), 0.0)
    prior = with_split(total[:, :128], total[:, 128:129] + total[:, 129:130], "hhl")
    prior_ref[0] = prior
    length = conv_ref.shape[0]
    kt = head_rows(kt_ref, h)
    conv = with_ones(conv_ref[...])
    inter = dot_tn(phi(qth_ref[...].astype(F32), 2.0), prior)
    causal = lax.broadcasted_iota(jnp.int32, (TILE, TILE), 0) >= lax.broadcasted_iota(
        jnp.int32, (TILE, TILE), 1
    )

    @pl.when(h == 0)
    def _():
        sums[...] = jnp.zeros_like(sums)
        den_ref[...] = jnp.zeros_like(den_ref)

    for t0 in range(0, length, TILE):
        q = q_ref[t0 : t0 + TILE]
        out = inter[t0 : t0 + TILE]
        d = dot(q, kt[:, t0 : t0 + TILE])
        w = jnp.where(causal, 1.0 + d * (0.25 + d * 0.03125), 0.0).astype(BF)
        out = out + dot(w, conv[t0 : t0 + TILE])
        if t0:
            d = dot(q, kt[:, :t0])
            w = (1.0 + d * (0.25 + d * 0.03125)).astype(BF)
            out = out + dot(w, conv[:t0])
        den = out[:, 128:129] + out[:, 130:131]
        att = out[:, :128] / den
        rows = slice(t0, t0 + TILE)
        att_ref[rows] = att
        lane = lanes(TILE)
        den_ref[rows] = jnp.where(lane == h, den, den_ref[rows])
        square = jnp.sum(att * att, axis=1, keepdims=True)
        agree = jnp.sum(
            att * (cot_ref[rows].astype(F32) * gain_ref[...]), axis=1, keepdims=True
        )
        sums[rows] += jnp.where(lane == 0, square, jnp.where(lane == 1, agree, 0.0))

    @pl.when(h == pl.num_programs(0) - 1)
    def _():
        stat_ref[...] = sums[...].T[:8]


def norm_kernel(
    width, att_ref, den_ref, stat_ref, cot_ref, gain_ref, qth_ref, normed_ref, dn_ref, back_ref
):
    h = pl.program_id(0)
    att = att_ref[...]
    gain = gain_ref[...]
    length = att.shape[0]
    den = jnp.sum(jnp.where(lanes(length) == h, den_ref[...], 0.0), axis=1, keepdims=True)
    inv = lax.rsqrt(stat_ref[:, 0:1] / width + EPS)
    shrink = inv * inv * inv * stat_ref[:, 1:2] / width
    normed_ref[...] = (att * inv * gain).astype(BF)
    d_att = inv * (cot_ref[...].astype(F32) * gain) - att * shrink
    each = 1.0 / den
    d_den = -jnp.sum(d_att * att, axis=1, keepdims=True) * each
    dn = with_split(d_att * each, d_den, "hlh")
    dn_ref[...] = dn
    total = dot(phi(qth_ref[...].astype(F32), 1.0), dn)
    back_ref[0] = with_split(total[:, :128], total[:, 128:129] + total[:, 129:130], "hl")


def backward_kernel(
    index_ref, all_ref, q_ref, k_ref, qt_ref, qth_ref, kth_ref, conv_ref, dn_ref, prior_ref,
    gq_ref, gk_ref, dconv_ref, acc_q, acc_kt, acc_k,
):
    h = pl.program_id(0)
    me = index_ref[0]
    total = jnp.zeros((ROWS, 256), F32)
    for j in range(all_ref.shape[0]):
        total = total + jnp.where(j > me, all_ref[j, 0].astype(F32), 0.0)
    later = with_split(total[:, :128], total[:, 128:129] + total[:, 129:130], "hl")
    length = conv_ref.shape[0]
    conv = with_ones(conv_ref[...])
    qt = head_rows(qt_ref, h)
    qm = head_lanes(q_ref, h)
    kth = kth_ref[...]
    kx = kth.astype(F32)
    qx = qth_ref[...].astype(F32)
    here = pl.ds(pl.multiple_of(h * FEAT, FEAT), FEAT)
    acc_q[here] = phi_grad(dot_nt(prior_ref[0], dn_ref[...]), qx)
    acc_kt[here] = phi_grad(dot_nt(later, conv), kx)
    inter = dot_tn(phi(kx, 2.0), later[:, :128])
    causal = lax.broadcasted_iota(jnp.int32, (TILE, TILE), 1) >= lax.broadcasted_iota(
        jnp.int32, (TILE, TILE), 0
    )

    @pl.when(h == 0)
    def _():
        acc_k[...] = jnp.zeros_like(acc_k)

    for s0 in range(0, length, TILE):
        rows = slice(s0, s0 + TILE)
        k = k_ref[rows]
        grad_c = inter[rows]
        grad_k = acc_k[rows]
        pieces = [slice(s0, s0 + TILE)]
        if s0 + TILE < length:
            pieces.append(slice(s0 + TILE, length))
        for at, cols in enumerate(pieces):
            d = dot(k, qt[:, cols])
            w = 1.0 + d * (0.25 + d * 0.03125)
            dk = dot_nt(conv[rows], dn_ref[cols]) * (0.25 + d * 0.0625)
            if at == 0:
                w = jnp.where(causal, w, 0.0)
                dk = jnp.where(causal, dk, 0.0)
            w = w.astype(BF)
            dk = dk.astype(BF)
            grad_c = grad_c + dot(w, dn_ref[cols, :128])
            grad_k = grad_k + dot(dk, qm[cols])
            acc_q[here, cols] += dot(kth[:, rows], dk)
        dconv_ref[rows] = grad_c.astype(BF)
        acc_k[rows] = grad_k

    @pl.when(h == pl.num_programs(0) - 1)
    def _():
        gq_ref[...] = acc_q[...].T.astype(BF)
        gk_ref[...] = (acc_k[...] + acc_kt[...].T).astype(BF)


def call(body, heads, in_specs, out_specs, out_shape, scratch=()):
    return pl.pallas_call(
        body,
        grid=(heads,),
        in_specs=in_specs,
        out_specs=out_specs,
        out_shape=out_shape,
        scratch_shapes=list(scratch),
        compiler_params=pltpu.CompilerParams(
            dimension_semantics=("arbitrary",), vmem_limit_bytes=LIMIT
        ),
    )


def shifted(block, axis, distance):
    size = lax.axis_size(axis)
    route = [(i - distance, i) for i in range(size) if 0 <= i - distance < size]
    return lax.ppermute(block, axis, route)


def per_device(width, queries, keys, values, conv_weight, gain, cotangent):
    length, channels = values.shape
    heads = queries.shape[1] // FEAT
    feats = heads * FEAT
    blocks = lax.axis_size("ctx")
    margin = CONV - 1
    shape = jax.ShapeDtypeStruct
    col = pl.BlockSpec((length, 128), lambda h: (0, h))
    wide = pl.BlockSpec((length, 256), lambda h: (0, h))
    tok = pl.BlockSpec((length, feats), lambda h: (0, 0))
    feat = pl.BlockSpec((feats, length), lambda h: (0, 0))
    mine = pl.BlockSpec((FEAT, length), lambda h: (h, 0))
    state = pl.BlockSpec((1, ROWS, 256), lambda h: (h, 0, 0))
    gathered = pl.BlockSpec((blocks, 1, ROWS, 256), lambda h: (0, h, 0, 0))
    vec = pl.BlockSpec((1, 128), lambda h: (0, h))
    pad = pl.BlockSpec((length, 128), lambda h: (0, 0))
    smem = pl.BlockSpec(memory_space=pltpu.SMEM)
    index = lax.axis_index("ctx").astype(jnp.int32).reshape(1)
    gain2 = gain.reshape(1, channels)
    previous = shifted(values[length - margin :], "ctx", 1).astype(F32)
    qt, kt = queries.T, keys.T

    conv, local = call(
        state_kernel,
        heads,
        [
            col,
            pl.BlockSpec((margin, 128), lambda h: (0, h)),
            pl.BlockSpec((CONV, 128), lambda h: (0, h)),
            mine,
        ],
        [col, state],
        [shape((length, channels), BF), shape((heads, ROWS, 256), BF)],
    )(values, previous, conv_weight, kt)
    before = lax.all_gather(local, "ctx")

    att, den, stat, prior = call(
        forward_kernel,
        heads,
        [smem, gathered, tok, feat, mine, col, col, vec],
        [col, pad, pl.BlockSpec((8, length), lambda h: (0, 0)), state],
        [
            shape((length, channels), F32),
            shape((length, 128), F32),
            shape((8, length), F32),
            shape((heads, ROWS, 256), BF),
        ],
        [pltpu.VMEM((length, 128), F32)],
    )(index, before, queries, kt, qt, conv, cotangent, gain2)
    stat = lax.psum(stat, "head").T

    normed, dn, back = call(
        functools.partial(norm_kernel, width),
        heads,
        [col, pad, pl.BlockSpec((length, 8), lambda h: (0, 0)), col, vec, mine],
        [col, wide, state],
        [
            shape((length, channels), BF),
            shape((length, heads * 256), BF),
            shape((heads, ROWS, 256), BF),
        ],
    )(att, den, stat, cotangent, gain2, qt)
    after = lax.all_gather(back, "ctx")

    grad_q, grad_k, d_conv = call(
        backward_kernel,
        heads,
        [smem, gathered, tok, tok, feat, mine, mine, col, wide, state],
        [tok, tok, col],
        [
            shape((length, feats), BF),
            shape((length, feats), BF),
            shape((length, channels), BF),
        ],
        [
            pltpu.VMEM((feats, length), F32),
            pltpu.VMEM((feats, length), F32),
            pltpu.VMEM((length, feats), F32),
        ],
    )(index, after, queries, keys, qt, qt, kt, conv, dn, prior)
    following = shifted(d_conv[:margin], "ctx", -1)
    extended = jnp.concatenate([d_conv, following], axis=0)
    total = jnp.zeros(values.shape, F32)
    for tap in range(CONV):
        total = total + conv_weight[tap] * extended[tap : tap + length]
    return (normed, grad_q, grad_k, total.astype(BF))


def solution(mesh):
    two = P("ctx", "head")

    def run(queries, keys, values, conv_weight, gain, cotangent):
        return jax.shard_map(
            functools.partial(per_device, values.shape[1]),
            mesh=mesh,
            in_specs=(two, two, two, P(None, "head"), P("head"), two),
            out_specs=(two, two, two, two),
            check_vma=False,
        )(queries, keys, values, conv_weight, gain, cotangent)

    return run
```

profile of v0, /device:TPU:1, one launch (start us, length us, event | category | flops | bytes accessed | tf_op | source)
XLA Modules:
  0.0 211.0 jit_solution(1214532340357987802)
XLA Ops:
  7.2 0.0 copy-start.1
  7.2 0.0 all-gather.5.cloned.1.call-start
  7.2 0.8 slice.21
  8.0 4.5 %collective-permute-start = (bf16[2,1024]{1,0:T(2,128)(2,1)S(1)}, bf16[2,1024]{1,0:T(2,128)(2,1)S(1)}, u32[]{:S(2)}, u32[]{:S(2)}) collective-permute-start(bf16[2,1024]{1,0:T(2,128)(2,1)S(1)} %slice.21), channel_id=1, source_target_pairs={{0,4},{4,8},{8,12},{12,16},{16,20},{20,24},{24,28},{1,5},{5,9},{9,... | collective-permute-start | bytes 12296 | tf_op jit(solution)/shard_map/ppermute | solution.py:246
  12.5 1.8 copy.13
  14.3 0.0 collective-permute-done
  14.3 0.6 convert_element_type.15.prev_ref
  14.9 7.2 %shard_map.93 = (bf16[1024,1024]{1,0:T(8,128)(2,1)}, bf16[8,160,256]{2,1,0:T(8,128)(2,1)}) custom-call(bf16[1024,1024]{1,0:T(8,128)(2,1)} %values_ref.1, f32[2,1024]{1,0:T(2,128)} %convert_element_type.15.prev_ref, f32[3,1024]{1,0:T(4,128)} %taps_ref.1, bf16[128,1024]{1,0:T(8,128)(2,1)} %bitcast.16), custom_call_target="tpu_custom_call" | custom-call | tf_op jit(solution)/shard_map/pallas_call | solution.py:271
  22.1 0.0 all-gather.5.cloned.1.call-update
  22.1 0.0 all-gather.7.cloned.1.call-start
  22.1 0.0 copy-done.1
  22.1 0.8 copy.14
  23.0 41.5 %all-gather.5.cloned.1.call-done = bf16[64,160,256]{2,1,0:T(8,128)(2,1)} async-done(((bf16[8,160,256]{2,1,0:T(8,128)(2,1)}), bf16[64,160,256]{2,1,0:T(8,128)(2,1)}) %all-gather.5.cloned.1.call-update) | async-done | bytes 5242896 | tf_op jit(solution)/shard_map/all_gather | solution.py:283
  64.5 20.6 %shard_map.94 = (f32[1024,1024]{1,0:T(8,128)}, f32[1024,128]{1,0:T(8,128)}, f32[8,1024]{1,0:T(8,128)}, bf16[8,160,256]{2,1,0:T(8,128)(2,1)}) custom-call(s32[1]{0:T(128)} %bitcast.index_ref, bf16[8,8,160,256]{3,2,1,0:T(8,128)(2,1)} %bitcast.14, bf16[1024,128]{1,0:T(8,128)(2,1)} %q_ref.3, bf16[128,1024]{1,0:T(8,128)(2,1)} %bitcast.17, ...), custom_call_target="tpu_custom_call" | custom-call | tf_op jit(solution)/shard_map/pallas_call | solution.py:285
  85.1 1.0 copy.15
  86.0 26.2 %psum.7.stat_ref = f32[1024,8]{1,0:T(8,128)} all-reduce(f32[1024,8]{1,0:T(8,128)S(1)} %bitcast.19), channel_id=1, replica_groups=mesh['ctx'=8,'head'=4] {'head'}, use_global_device_ids=true, to_apply=%region_0.0 | all-reduce | flops 8192 | bytes 65536 | tf_op jit(solution)/shard_map/psum | solution.py:298
  112.2 0.0 copy-start.2
  112.2 12.3 %shard_map.95 = (bf16[1024,1024]{1,0:T(8,128)(2,1)}, bf16[1024,2048]{1,0:T(8,128)(2,1)}, bf16[8,160,256]{2,1,0:T(8,128)(2,1)}) custom-call(f32[1024,1024]{1,0:T(8,128)} %get-tuple-element.18.att_ref, f32[1024,128]{1,0:T(8,128)} %get-tuple-element.19.den_ref, f32[1024,8]{1,0:T(8,128)} %psum.7.stat_ref, bf16[1024,1024]{1,0:T(8,128)(2,1)} %cot_ref.3, ...), custom_call_target="tpu_custom_call" | custom-call | tf_op jit(solution)/shard_map/pallas_call | solution.py:300
  124.5 0.0 all-gather.7.cloned.1.call-update
  124.5 0.0 copy-done.2
  124.5 43.4 %all-gather.7.cloned.1.call-done = bf16[64,160,256]{2,1,0:T(8,128)(2,1)} async-done(((bf16[8,160,256]{2,1,0:T(8,128)(2,1)}), bf16[64,160,256]{2,1,0:T(8,128)(2,1)}) %all-gather.7.cloned.1.call-update) | async-done | bytes 5242896 | tf_op jit(solution)/shard_map/all_gather | solution.py:311
  167.9 27.5 %shard_map.96 = (bf16[1024,128]{1,0:T(8,128)(2,1)}, bf16[1024,128]{1,0:T(8,128)(2,1)}, bf16[1024,1024]{1,0:T(8,128)(2,1)}) custom-call(s32[1]{0:T(128)} %bitcast.index_ref, bf16[8,8,160,256]{3,2,1,0:T(8,128)(2,1)} %bitcast.15, bf16[1024,128]{1,0:T(8,128)(2,1)} %q_ref.3, bf16[1024,128]{1,0:T(8,128)(2,1)} %k_ref.1, bf16[128,1024]{1,0:T(8,128)(2,1)} %bitcast.12, ...), custom_call_target="tpu_custom_call" | custom-call | tf_op jit(solution)/shard_map/pallas_call | solution.py:313
  195.4 0.0 copy-start
  195.4 0.9 slice.24
  196.3 2.2 %collective-permute-start.1 = (bf16[2,1024]{1,0:T(2,128)(2,1)S(1)}, bf16[2,1024]{1,0:T(2,128)(2,1)S(1)}, u32[]{:S(2)}, u32[]{:S(2)}) collective-permute-start(bf16[2,1024]{1,0:T(2,128)(2,1)S(1)} %slice.24), channel_id=1, source_target_pairs={{4,0},{8,4},{12,8},{16,12},{20,16},{24,20},{28,24},{5,1},{9,5},{13... | collective-permute-start | bytes 12296 | tf_op jit(solution)/shard_map/ppermute | solution.py:246
  198.5 1.8 constant_dynamic-update-slice_fusion.1
  200.2 1.0 collective-permute-done.1
  201.2 0.0 copy-done
  201.3 2.9 %add_convert_fusion = bf16[1024,1024]{1,0:T(8,128)(2,1)} fusion(bf16[1024,1024]{1,0:T(8,128)(2,1)S(1)} %copy-done, bf16[1026,1024]{1,0:T(8,128)(2,1)S(1)} %constant_dynamic-update-slice_fusion, f32[1024]{0:T(1024)S(1)} %bitcast.23, f32[1024]{0:T(1024)S(1)} %bitcast.24, f32[1024]{0:T(1024)S(1)} %bitcast.22), kind=kLoop, calls=%fused_computation | loop fusion | flops 9437184 | bytes 8400896 | tf_op jit(solution)/shard_map/convert_element_type | solution.py:334
  (2 shorter events, 0.0 us)
Async XLA Ops:
  7.2 15.0 %copy-start.1 = (bf16[1024,128]{1,0:T(8,128)(2,1)S(1)}, bf16[1024,128]{1,0:T(8,128)(2,1)}, u32[]{:S(2)}) copy-start(bf16[1024,128]{1,0:T(8,128)(2,1)} %q_ref.3) | copy-start | bytes 786436
  7.2 57.3 %all-gather.5.cloned.1.call-start = ((), (), s32[]{:S(2)}) async-start(), calls=%async_computation | async-start | bytes 5898240 | tf_op jit(solution)/shard_map/all_gather | solution.py:283
  8.0 6.3 %collective-permute-start = (bf16[2,1024]{1,0:T(2,128)(2,1)S(1)}, bf16[2,1024]{1,0:T(2,128)(2,1)S(1)}, u32[]{:S(2)}, u32[]{:S(2)}) collective-permute-start(bf16[2,1024]{1,0:T(2,128)(2,1)S(1)} %slice.21), channel_id=1, source_target_pairs={{0,4},{4,8},{8,12},{12,16},{16,20},{20,24},{24,28},{1,5},{5,9},{9,... | collective-permute-start | bytes 12296 | tf_op jit(solution)/shard_map/ppermute | solution.py:246
  22.1 145.8 %all-gather.7.cloned.1.call-start = ((), (), s32[]{:S(2)}) async-start(), calls=%async_computation.1 | async-start | bytes 5898240 | tf_op jit(solution)/shard_map/all_gather | solution.py:311
  112.2 12.3 %copy-start.2 = (f32[3,1024]{1,0:T(4,128)S(1)}, f32[3,1024]{1,0:T(4,128)}, u32[]{:S(2)}) copy-start(f32[3,1024]{1,0:T(4,128)} %taps_ref.1) | copy-start | bytes 36868
  195.4 5.8 %copy-start = (bf16[1024,1024]{1,0:T(8,128)(2,1)S(1)}, bf16[1024,1024]{1,0:T(8,128)(2,1)}, u32[]{:S(2)}) copy-start(bf16[1024,1024]{1,0:T(8,128)(2,1)} %get-tuple-element.27) | copy-start | bytes 6291460
  196.3 4.9 %collective-permute-start.1 = (bf16[2,1024]{1,0:T(2,128)(2,1)S(1)}, bf16[2,1024]{1,0:T(2,128)(2,1)S(1)}, u32[]{:S(2)}, u32[]{:S(2)}) collective-permute-start(bf16[2,1024]{1,0:T(2,128)(2,1)S(1)} %slice.24), channel_id=1, source_target_pairs={{4,0},{8,4},{12,8},{16,12},{20,16},{24,20},{28,24},{5,1},{9,5},{13... | collective-permute-start | bytes 12296 | tf_op jit(solution)/shard_map/ppermute | solution.py:246
Sparse Core Ops, SparseCore 0:
  22.2 42.2 all-gather.4
  124.6 43.2 all-gather.6
where the time goes:
time: 212 us; the launch traced here: 211 us
  waiting for transfers between devices  85.9 us (41%)
  Pallas kernels  67.5 us (32%)
  blocking collectives  26.2 us (12%)
  between operations  14.1 us (7%)
  local copies, waits for them, and re-layouts  7.02 us (3%)
  starting transfers between devices  6.73 us (3%)
  other arithmetic  3.52 us (2%)
    all_gather x1, waiting for transfers between devices, per_device(): after = lax.all_gather(back, 'ctx')  43.4 us
    all_gather x1, waiting for transfers between devices, per_device(): before = lax.all_gather(local, 'ctx')  41.5 us
    pallas_call x1, Pallas kernels, per_device(): call(backward_kernel, heads, [smem, gathered, tok, tok, feat, mine, mine,...  27.5 us
    psum x1, blocking collectives, per_device(): stat = lax.psum(stat, 'head').T  26.2 us
    pallas_call x1, Pallas kernels, per_device(): call(forward_kernel, heads, [smem, gathered, tok, feat, mine, col, col, v...  20.6 us
    pallas_call x1, Pallas kernels, per_device(): call(functools.partial(norm_kernel, width), heads, [col, pad, pl.BlockSpe...  12.3 us
    pallas_call x1, Pallas kernels, per_device(): call(state_kernel, heads, [col, pl.BlockSpec((margin, 128), lambda h: (0,...  7.18 us
    ppermute x2, starting transfers between devices, shifted(): return lax.ppermute(block, axis, route)  6.65 us
  transfers between devices with their start and end apart: 4, of which 3 were waited for; matrix products, arithmetic and copies ran while one was open for 2% of the time, Pallas kernels for 0%

commit v1 on v0

v1 whole, which is shorter than its diff:
```python
import functools
import math

import jax
import jax.numpy as jnp
from jax import lax
from jax.experimental import pallas as pl
from jax.experimental.pallas import tpu as pltpu
from jax.sharding import PartitionSpec as P

FEAT = 16
CONV = 3
ROWS = 160
TILE = 256
S = 0.25 / math.sqrt(2.0)
EPS = 1e-06
F32 = jnp.float32
BF = jnp.bfloat16
LIMIT = 56 * 1024 * 1024


def dot(a, b):
    return jnp.dot(a, b, preferred_element_type=F32)


def dot_nt(a, b):
    return lax.dot_general(a, b, (((1,), (1,)), ((), ())), preferred_element_type=F32)


def dot_tn(a, b):
    return lax.dot_general(a, b, (((0,), (0,)), ((), ())), preferred_element_type=F32)


def turned(x, d):
    return pltpu.roll(x, FEAT - d, 0)


def phi(x, pair):
    parts = [x * 0.5, (x * x) * S]
    for d in range(1, 8):
        parts.append((x * turned(x, d)) * (pair * S))
    parts.append((x[:8] * x[8:]) * (pair * S))
    row = lax.broadcasted_iota(jnp.int32, (8, x.shape[1]), 0)
    parts.append(jnp.where(row == 0, 1.0, 0.0).astype(F32))
    return jnp.concatenate(parts, axis=0).astype(BF)


def phi_grad(g, x):
    total = g[16:32] * x
    for d in range(1, 8):
        part = g[16 + 16 * d : 32 + 16 * d]
        total = total + part * turned(x, d) + pltpu.roll(part * x, d, 0)
    last = g[144:152]
    total = total + jnp.concatenate([last * x[8:], last * x[:8]], axis=0)
    return g[:16] * 0.5 + (2.0 * S) * total


def lanes(rows):
    return lax.broadcasted_iota(jnp.int32, (rows, 128), 1)


def with_ones(conv):
    ones = jnp.where(lanes(conv.shape[0]) < 2, 1.0, 0.0).astype(BF)
    return jnp.concatenate([conv, ones], axis=1)


def with_split(wide, column, order):
    high = column.astype(BF).astype(F32)
    low = column - high
    lane = lanes(wide.shape[0])
    right = jnp.zeros(lane.shape, F32)
    for at, kind in enumerate(order):
        right = jnp.where(lane == at, high if kind == "h" else low, right)
    return jnp.concatenate([wide.astype(BF), right.astype(BF)], axis=1)


def put_sum(sum_ref, h, column):
    @pl.when(h == 0)
    def _():
        sum_ref[...] = jnp.zeros_like(sum_ref)

    sum_ref[...] = jnp.where(lanes(ROWS) == h, column, sum_ref[...])


def state_kernel(values_ref, prev_ref, taps_ref, kt_ref, conv_ref, state_ref, sum_ref):
    v = values_ref[...].astype(F32)
    row = lax.broadcasted_iota(jnp.int32, v.shape, 0)
    one = jnp.where(row == 0, prev_ref[1:2], pltpu.roll(v, 1, 0))
    two = jnp.where(
        row == 0, prev_ref[0:1], jnp.where(row == 1, prev_ref[1:2], pltpu.roll(v, 2, 0))
    )
    conv = (taps_ref[0:1] * v + taps_ref[1:2] * one + taps_ref[2:3] * two).astype(BF)
    conv_ref[...] = conv
    total = dot(phi(kt_ref[...].astype(F32), 1.0), with_ones(conv))
    state_ref[0] = total[:, :128].astype(BF)
    put_sum(sum_ref, pl.program_id(0), total[:, 128:129])


class Exchange:
    def __init__(self, sign, blocks, state_ref, sum_ref, refs):
        self.sign, self.blocks, self.chips = sign, blocks, blocks // 2
        self.state_ref, self.sum_ref = state_ref, sum_ref
        self.states, self.sums, self.acc, self.give, self.got = refs[:5]
        self.send, self.recv, self.swap_send, self.swap_recv = refs[5:]
        self.me = lax.axis_index("ctx")
        self.chip, self.core = self.me // 2, self.me % 2

    def greet(self, peers=0):
        barrier = pltpu.get_barrier_semaphore()
        for d in range(1, self.chips):
            other = (self.me + 2 * d) % self.blocks
            pl.semaphore_signal(barrier, inc=1, device_id={"ctx": other})
        pl.semaphore_signal(barrier, inc=1, device_id={"ctx": self.me + 1 - 2 * self.core})
        for d in range(1, peers):
            other = (lax.axis_index("head") + d) % peers
            pl.semaphore_signal(barrier, inc=1, device_id={"head": other})
        pl.semaphore_wait(barrier, self.chips + max(peers - 1, 0))

    def copies(self, d):
        to = (self.me + 2 * d * self.sign + self.blocks) % self.blocks
        pairs = [(self.state_ref, self.states), (self.sum_ref, self.sums)]
        return [
            pltpu.make_async_remote_copy(
                src_ref=src,
                dst_ref=dst.at[d - 1],
                send_sem=self.send.at[d - 1, k],
                recv_sem=self.recv.at[d - 1, k],
                device_id={"ctx": to},
            )
            for k, (src, dst) in enumerate(pairs)
        ]

    def swap(self):
        return pltpu.make_async_remote_copy(
            src_ref=self.give,
            dst_ref=self.got,
            send_sem=self.swap_send,
            recv_sem=self.swap_recv,
            device_id={"ctx": self.me + 1 - 2 * self.core},
        )

    def reaches(self, d):
        return self.chip + d < self.chips if self.sign > 0 else self.chip >= d

    def reached(self, d):
        return self.chip >= d if self.sign > 0 else self.chip + d < self.chips

    def start(self):
        for d in range(1, self.chips):

            @pl.when(self.reaches(d))
            def _():
                for copy in self.copies(d):
                    copy.start()

    def merge(self):
        heads = self.state_ref.shape[0]
        self.acc[...] = jnp.zeros_like(self.acc)
        for d in range(1, self.chips):

            @pl.when(self.reached(d))
            def _():
                for copy in self.copies(d):
                    copy.wait_recv()
                self.acc[:heads] += self.states[d - 1].astype(F32)
                self.acc[heads] += self.sums[d - 1]

        self.give[...] = self.acc[...]

        @pl.when(self.core == (0 if self.sign > 0 else 1))
        def _():
            self.give[:heads] += self.state_ref[...].astype(F32)
            self.give[heads] += self.sum_ref[...]

        self.swap().start()

    def finish(self, out, order):
        heads = self.state_ref.shape[0]
        self.swap().wait()
        for d in range(1, self.chips):

            @pl.when(self.reaches(d))
            def _():
                for copy in self.copies(d):
                    copy.wait_send()

        sums = self.acc[heads] + self.got[heads]
        for h in range(heads):
            column = jnp.sum(jnp.where(lanes(ROWS) == h, sums, 0.0), axis=1, keepdims=True)
            out[h] = with_split(self.acc[h] + self.got[h], column, order)


def exchange_scratch(blocks, heads):
    slots = max(blocks // 2 - 1, 1)
    return [
        pltpu.VMEM((slots, heads, ROWS, 128), BF),
        pltpu.VMEM((slots, ROWS, 128), F32),
        pltpu.VMEM((heads + 1, ROWS, 128), F32),
        pltpu.VMEM((heads + 1, ROWS, 128), F32),
        pltpu.VMEM((heads + 1, ROWS, 128), F32),
        pltpu.SemaphoreType.DMA((slots, 2)),
        pltpu.SemaphoreType.DMA((slots, 2)),
        pltpu.SemaphoreType.DMA,
        pltpu.SemaphoreType.DMA,
    ]


def head_rows(ref, h):
    row = lax.broadcasted_iota(jnp.int32, (ref.shape[0], 1), 0)
    return (ref[...].astype(F32) * jnp.where(row // FEAT == h, 1.0, 0.0)).astype(BF)


def head_lanes(ref, h):
    lane = lax.broadcasted_iota(jnp.int32, (1, ref.shape[1]), 1)
    return (ref[...].astype(F32) * jnp.where(lane // FEAT == h, 1.0, 0.0)).astype(BF)


def forward_kernel(
    blocks, peers, heads,
    state_ref, sum_ref, q_ref, kt_ref, qth_ref, conv_ref, cot_ref, gain_ref,
    att_ref, den_ref, stat_ref, prior_ref,
    sums, numer, stat, stats, stat_send, stat_recv, *refs,
):
    step = pl.program_id(0)
    h = step % heads
    exchange = Exchange(1, blocks, state_ref, sum_ref, refs)
    length = conv_ref.shape[0]

    @pl.when(step == 0)
    def _():
        exchange.greet(peers)
        exchange.start()
        sums[...] = jnp.zeros_like(sums)
        den_ref[...] = jnp.zeros_like(den_ref)

    @pl.when(step == heads - 1)
    def _():
        exchange.merge()

    @pl.when(step == heads)
    def _():
        exchange.finish(prior_ref, "hhl")

    @pl.when(step < heads)
    def _():
        kt = head_rows(kt_ref, h)
        conv = with_ones(conv_ref[...])
        causal = lax.broadcasted_iota(jnp.int32, (TILE, TILE), 0) >= lax.broadcasted_iota(
            jnp.int32, (TILE, TILE), 1
        )
        for t0 in range(0, length, TILE):
            q = q_ref[t0 : t0 + TILE]
            d = dot(q, kt[:, t0 : t0 + TILE])
            w = jnp.where(causal, 1.0 + d * (0.25 + d * 0.03125), 0.0).astype(BF)
            out = dot(w, conv[t0 : t0 + TILE])
            if t0:
                d = dot(q, kt[:, :t0])
                w = (1.0 + d * (0.25 + d * 0.03125)).astype(BF)
                out = out + dot(w, conv[:t0])
            numer[h, t0 : t0 + TILE] = out

    @pl.when(step >= heads)
    def _():
        out = numer[h] + dot_tn(phi(qth_ref[...].astype(F32), 2.0), prior_ref[h])
        den = out[:, 128:129] + out[:, 130:131]
        att = out[:, :128] / den
        att_ref[...] = att
        lane = lanes(length)
        den_ref[...] = jnp.where(lane == h, den, den_ref[...])
        square = jnp.sum(att * att, axis=1, keepdims=True)
        agree = jnp.sum(
            att * (cot_ref[...].astype(F32) * gain_ref[...]), axis=1, keepdims=True
        )
        sums[...] += jnp.where(lane == 0, square, jnp.where(lane == 1, agree, 0.0))

    @pl.when(step == 2 * heads - 1)
    def _():
        stat[...] = sums[...].T[:8]
        mine = lax.axis_index("head")
        copies = [
            pltpu.make_async_remote_copy(
                src_ref=stat,
                dst_ref=stats.at[d - 1],
                send_sem=stat_send.at[d - 1],
                recv_sem=stat_recv.at[d - 1],
                device_id={"head": (mine + d) % peers},
            )
            for d in range(1, peers)
        ]
        for copy in copies:
            copy.start()
        total = stat[...]
        for d, copy in enumerate(copies):
            copy.wait()
            total = total + stats[d]
        stat_ref[...] = jnp.concatenate([total] * 16, axis=0).T


def norm_kernel(
    width, att_ref, den_ref, stat_ref, cot_ref, gain_ref, qth_ref, normed_ref, dn_ref, back_ref,
    sum_ref,
):
    h = pl.program_id(0)
    att = att_ref[...]
    gain = gain_ref[...]
    length = att.shape[0]
    den = jnp.sum(jnp.where(lanes(length) == h, den_ref[...], 0.0), axis=1, keepdims=True)
    inv = lax.rsqrt(stat_ref[:, 0:1] / width + EPS)
    shrink = inv * inv * inv * stat_ref[:, 1:2] / width
    normed_ref[...] = (att * inv * gain).astype(BF)
    d_att = inv * (cot_ref[...].astype(F32) * gain) - att * shrink
    each = 1.0 / den
    d_den = -jnp.sum(d_att * att, axis=1, keepdims=True) * each
    dn = with_split(d_att * each, d_den, "hlh")
    dn_ref[...] = dn
    total = dot(phi(qth_ref[...].astype(F32), 1.0), dn)
    back_ref[0] = total[:, :128].astype(BF)
    put_sum(sum_ref, h, total[:, 128:129] + total[:, 129:130])


def backward_kernel(
    blocks, heads,
    state_ref, sum_ref, q_ref, k_ref, qt_ref, qth_ref, kth_ref, conv_ref, dn_ref, prior_ref,
    gq_ref, gk_ref, dconv_ref, acc_q, acc_kt, acc_k, grad_c, later, *refs,
):
    step = pl.program_id(0)
    h = step % heads
    exchange = Exchange(-1, blocks, state_ref, sum_ref, refs)
    length = conv_ref.shape[0]
    here = pl.ds(pl.multiple_of(h * FEAT, FEAT), FEAT)

    @pl.when(step == 0)
    def _():
        exchange.greet()
        exchange.start()
        acc_k[...] = jnp.zeros_like(acc_k)

    @pl.when(step == heads - 1)
    def _():
        exchange.merge()

    @pl.when(step == heads)
    def _():
        exchange.finish(later, "hl")

    @pl.when(step < heads)
    def _():
        conv = with_ones(conv_ref[...])
        qt = head_rows(qt_ref, h)
        qm = head_lanes(q_ref, h)
        kth = kth_ref[...]
        acc_q[here] = phi_grad(dot_nt(prior_ref[0], dn_ref[...]), qth_ref[...].astype(F32))
        causal = lax.broadcasted_iota(jnp.int32, (TILE, TILE), 1) >= lax.broadcasted_iota(
            jnp.int32, (TILE, TILE), 0
        )
        for s0 in range(0, length, TILE):
            rows = slice(s0, s0 + TILE)
            k = k_ref[rows]
            total_c = jnp.zeros((TILE, 128), F32)
            total_k = acc_k[rows]
            pieces = [slice(s0, s0 + TILE)]
            if s0 + TILE < length:
                pieces.append(slice(s0 + TILE, length))
            for at, cols in enumerate(pieces):
                d = dot(k, qt[:, cols])
                w = 1.0 + d * (0.25 + d * 0.03125)
                dk = dot_nt(conv[rows], dn_ref[cols]) * (0.25 + d * 0.0625)
                if at == 0:
                    w = jnp.where(causal, w, 0.0)
                    dk = jnp.where(causal, dk, 0.0)
                w = w.astype(BF)
                dk = dk.astype(BF)
                total_c = total_c + dot(w, dn_ref[cols, :128])
                total_k = total_k + dot(dk, qm[cols])
                acc_q[here, cols] += dot(kth[:, rows], dk)
            grad_c[h, rows] = total_c
            acc_k[rows] = total_k

    @pl.when(step >= heads)
    def _():
        kx = kth_ref[...].astype(F32)
        acc_kt[here] = phi_grad(dot_nt(later[h], with_ones(conv_ref[...])), kx)
        inter = dot_tn(phi(kx, 2.0), later[h, :, :128])
        dconv_ref[...] = (grad_c[h] + inter).astype(BF)

    @pl.when(step == 2 * heads - 1)
    def _():
        gq_ref[...] = acc_q[...].T.astype(BF)
        gk_ref[...] = (acc_k[...] + acc_kt[...].T).astype(BF)


def call(body, steps, in_specs, out_specs, out_shape, scratch=(), collective_id=None):
    remote = {} if collective_id is None else dict(
        collective_id=collective_id, has_side_effects=True
    )
    return pl.pallas_call(
        body,
        grid=(steps,),
        in_specs=in_specs,
        out_specs=out_specs,
        out_shape=out_shape,
        scratch_shapes=list(scratch),
        compiler_params=pltpu.CompilerParams(
            dimension_semantics=("arbitrary",), vmem_limit_bytes=LIMIT, **remote
        ),
    )


def shifted(block, axis, distance):
    size = lax.axis_size(axis)
    route = [(i - distance, i) for i in range(size) if 0 <= i - distance < size]
    return lax.ppermute(block, axis, route)


def per_device(width, queries, keys, values, conv_weight, gain, cotangent):
    length, channels = values.shape
    heads = queries.shape[1] // FEAT
    feats = heads * FEAT
    blocks = lax.axis_size("ctx")
    margin = CONV - 1
    shape = jax.ShapeDtypeStruct
    peers = lax.axis_size("head")
    col = pl.BlockSpec((length, 128), lambda h: (0, h))
    wide = pl.BlockSpec((length, 256), lambda h: (0, h))
    tok = pl.BlockSpec((length, feats), lambda h: (0, 0))
    feat = pl.BlockSpec((feats, length), lambda h: (0, 0))
    mine = pl.BlockSpec((FEAT, length), lambda h: (h, 0))
    state = pl.BlockSpec((1, ROWS, 128), lambda h: (h, 0, 0))
    states = pl.BlockSpec((heads, ROWS, 128), lambda h: (0, 0, 0))
    priors = pl.BlockSpec((heads, ROWS, 256), lambda h: (0, 0, 0))
    sums = pl.BlockSpec((ROWS, 128), lambda h: (0, 0))
    vec = pl.BlockSpec((1, 128), lambda h: (0, h))
    pad = pl.BlockSpec((length, 128), lambda h: (0, 0))

    def early(i):
        return i % heads * (1 - i // heads) + i // heads * (heads - 1)

    def late(i):
        return i // heads * (i % heads)

    gain2 = gain.reshape(1, channels)
    previous = shifted(values[length - margin :], "ctx", 1).astype(F32)
    qt, kt = queries.T, keys.T

    conv, local, local_sum = call(
        state_kernel,
        heads,
        [
            col,
            pl.BlockSpec((margin, 128), lambda h: (0, h)),
            pl.BlockSpec((CONV, 128), lambda h: (0, h)),
            mine,
        ],
        [col, state, sums],
        [
            shape((length, channels), BF),
            shape((heads, ROWS, 128), BF),
            shape((ROWS, 128), F32),
        ],
    )(values, previous, conv_weight, kt)

    att, den, stat, prior = call(
        functools.partial(forward_kernel, blocks, peers, heads),
        2 * heads,
        [
            states,
            sums,
            tok,
            feat,
            pl.BlockSpec((FEAT, length), lambda i: (late(i), 0)),
            pl.BlockSpec((length, 128), lambda i: (0, early(i))),
            pl.BlockSpec((length, 128), lambda i: (0, late(i))),
            pl.BlockSpec((1, 128), lambda i: (0, late(i))),
        ],
        [pl.BlockSpec((length, 128), lambda i: (0, late(i))), pad, pad, priors],
        [
            shape((length, channels), F32),
            shape((length, 128), F32),
            shape((length, 128), F32),
            shape((heads, ROWS, 256), BF),
        ],
        [
            pltpu.VMEM((length, 128), F32),
            pltpu.VMEM((heads, length, 256), F32),
            pltpu.VMEM((8, length), F32),
            pltpu.VMEM((max(peers - 1, 1), 8, length), F32),
            pltpu.SemaphoreType.DMA((max(peers - 1, 1),)),
            pltpu.SemaphoreType.DMA((max(peers - 1, 1),)),
        ]
        + exchange_scratch(blocks, heads),
        0,
    )(local, local_sum, queries, kt, qt, conv, cotangent, gain2)

    normed, dn, back, back_sum = call(
        functools.partial(norm_kernel, width),
        heads,
        [col, pad, pad, col, vec, mine],
        [col, wide, state, sums],
        [
            shape((length, channels), BF),
            shape((length, heads * 256), BF),
            shape((heads, ROWS, 128), BF),
            shape((ROWS, 128), F32),
        ],
    )(att, den, stat, cotangent, gain2, qt)

    grad_q, grad_k, d_conv = call(
        functools.partial(backward_kernel, blocks, heads),
        2 * heads,
        [
            states,
            sums,
            tok,
            tok,
            feat,
            pl.BlockSpec((FEAT, length), lambda i: (early(i), 0)),
            pl.BlockSpec((FEAT, length), lambda i: (i % heads, 0)),
            pl.BlockSpec((length, 128), lambda i: (0, i % heads)),
            pl.BlockSpec((length, 256), lambda i: (0, early(i))),
            pl.BlockSpec((1, ROWS, 256), lambda i: (early(i), 0, 0)),
        ],
        [tok, tok, pl.BlockSpec((length, 128), lambda i: (0, late(i)))],
        [
            shape((length, feats), BF),
            shape((length, feats), BF),
            shape((length, channels), BF),
        ],
        [
            pltpu.VMEM((feats, length), F32),
            pltpu.VMEM((feats, length), F32),
            pltpu.VMEM((length, feats), F32),
            pltpu.VMEM((heads, length, 128), F32),
            pltpu.VMEM((heads, ROWS, 256), BF),
        ]
        + exchange_scratch(blocks, heads),
        1,
    )(back, back_sum, queries, keys, qt, qt, kt, conv, dn, prior)
    following = shifted(d_conv[:margin], "ctx", -1)
    extended = jnp.concatenate([d_conv, following], axis=0)
    total = jnp.zeros(values.shape, F32)
    for tap in range(CONV):
        total = total + conv_weight[tap] * extended[tap : tap + length]
    return (normed, grad_q, grad_k, total.astype(BF))


def solution(mesh):
    two = P("ctx", "head")

    def run(queries, keys, values, conv_weight, gain, cotangent):
        return jax.shard_map(
            functools.partial(per_device, values.shape[1]),
            mesh=mesh,
            in_specs=(two, two, two, P(None, "head"), P("head"), two),
            out_specs=(two, two, two, two),
            check_vma=False,
        )(queries, keys, values, conv_weight, gain, cotangent)

    return run
```

time: 212 us -> 116 us (0.55)
  waiting for transfers between devices: 85.9 us -> 0.34 us
  blocking collectives: 26.2 us -> 0 us
  Pallas kernels: 67.5 us -> 93.4 us
  between operations: 14.1 us -> 0.71 us
  local copies, waits for them, and re-layouts: 7.02 us -> 9.22 us
    all_gather x2 -> x0, waiting for transfers between devices: 84.9 us -> none  [the longest x1 43.4 us: per_device(): after = lax.all_gather(back, 'ctx')]
    psum x1 -> x0, blocking collectives: 26.2 us -> none  [per_device(): stat = lax.psum(stat, 'head').T]
    pallas_call x3, Pallas kernels: 60.4 us -> 86.2 us  [the longest x1 37.4 us: per_device(): call(functools.partial(backward_kernel, blocks, heads), 2 * heads, [state...]
    unnamed x9 -> x11, local copies, waits for them, and re-layouts: 4.41 us -> 6.76 us
  transfers between devices with their start and end apart: 4 -> 2, of which waited for: 3 -> 1; matrix products, arithmetic and copies ran while one was open for 2% -> 5% of each run, Pallas kernels for 0% -> 0%
where the time goes in v1:
time: 116 us; the launch traced here: 114 us
  Pallas kernels  93.4 us (81%)
  local copies, waits for them, and re-layouts  9.22 us (8%)
  starting transfers between devices  7.3 us (6%)
  other arithmetic  3.52 us (3%)
    pallas_call x1, Pallas kernels, per_device(): call(functools.partial(backward_kernel, blocks, heads), 2 * heads, [state...  37.4 us
    pallas_call x1, Pallas kernels, per_device(): call(functools.partial(forward_kernel, blocks, peers, heads), 2 * heads,...  36 us
    pallas_call x1, Pallas kernels, per_device(): call(functools.partial(norm_kernel, width), heads, [col, pad, pad, col, v...  12.8 us
    ppermute x2, starting transfers between devices, shifted(): return lax.ppermute(block, axis, route)  7.3 us
    pallas_call x1, Pallas kernels, per_device(): call(state_kernel, heads, [col, pl.BlockSpec((margin, 128), lambda h: (0,...  7.16 us
    unnamed x11, local copies, waits for them, and re-layouts  6.76 us
    convert_element_type x1, other arithmetic, per_device(): return (normed, grad_q, grad_k, total.astype(BF))  2.92 us
  transfers between devices with their start and end apart: 2, of which 1 were waited for; matrix products, arithmetic and copies ran while one was open for 5% of the time, Pallas kernels for 0%

profile of v1, /device:TPU:1, one launch (start us, length us, event | category | flops | bytes accessed | tf_op | source)
XLA Modules:
  0.0 114.5 jit_solution(16424019222067982589)
XLA Ops:
  0.6 0.7 slice.21
  1.4 4.5 %collective-permute-start = (bf16[2,1024]{1,0:T(2,128)(2,1)S(1)}, bf16[2,1024]{1,0:T(2,128)(2,1)S(1)}, u32[]{:S(2)}, u32[]{:S(2)}) collective-permute-start(bf16[2,1024]{1,0:T(2,128)(2,1)S(1)} %slice.21), channel_id=1, source_target_pairs={{0,4},{4,8},{8,12},{12,16},{16,20},{20,24},{24,28},{1,5},{5,9},{9,... | collective-permute-start | bytes 12296 | tf_op jit(solution)/shard_map/ppermute | solution.py:412
  5.9 0.8 fusion
  6.7 1.8 %copy.10 = bf16[1024,128]{0,1:T(8,128)(2,1)} copy(bf16[1024,128]{1,0:T(8,128)(2,1)} %k_ref.1) | data formatting | bytes 524288 | tf_op args[1]
  8.5 1.8 %copy.11 = bf16[1024,128]{0,1:T(8,128)(2,1)} copy(bf16[1024,128]{1,0:T(8,128)(2,1)} %q_ref.3) | data formatting | bytes 524288 | tf_op args[0]
  10.3 0.0 collective-permute-done
  10.3 0.6 convert_element_type.15.prev_ref
  10.9 7.2 %shard_map.93 = (bf16[1024,1024]{1,0:T(8,128)(2,1)}, bf16[8,160,128]{2,1,0:T(8,128)(2,1)}, f32[160,128]{1,0:T(8,128)}) custom-call(bf16[1024,1024]{1,0:T(8,128)(2,1)} %values_ref.1, f32[2,1024]{1,0:T(2,128)} %convert_element_type.15.prev_ref, f32[3,1024]{1,0:T(4,128)} %taps_ref.1, bf16[128,1024]{1,0:T(8,128)(2,1)} %bitcast.10), custom_call_target="tpu_custom_call" | custom-call | tf_op jit(solution)/shard_map/pallas_call | solution.py:445
  18.1 36.0 %shard_map.94 = (f32[1024,1024]{1,0:T(8,128)}, f32[1024,128]{1,0:T(8,128)}, f32[1024,128]{1,0:T(8,128)}, bf16[8,160,256]{2,1,0:T(8,128)(2,1)}) custom-call(bf16[8,160,128]{2,1,0:T(8,128)(2,1)} %get-tuple-element.18.state_ref, f32[160,128]{1,0:T(8,128)} %get-tuple-element.19.sum_ref, bf16[1024,128]{1,0:T(8,128)(2,1)} %q_ref.3, bf16[128,1024]{1,0:T(8,128)(2,1)} %bitcast.11, ...), custom_call_target="tpu_custom_call" | custom-call | tf_op jit(solution)/shard_map/pallas_call | solution.py:462
  54.1 12.8 %shard_map.95 = (bf16[1024,1024]{1,0:T(8,128)(2,1)}, bf16[1024,2048]{1,0:T(8,128)(2,1)}, bf16[8,160,128]{2,1,0:T(8,128)(2,1)}, f32[160,128]{1,0:T(8,128)}) custom-call(f32[1024,1024]{1,0:T(8,128)} %get-tuple-element.21.att_ref, f32[1024,128]{1,0:T(8,128)} %get-tuple-element.22.den_ref, f32[1024,128]{1,0:T(8,128)} %get-tuple-element.23.stat_ref, ...), custom_call_target="tpu_custom_call" | custom-call | tf_op jit(solution)/shard_map/pallas_call | solution.py:494
  66.9 37.4 %shard_map.96 = (bf16[1024,128]{1,0:T(8,128)(2,1)}, bf16[1024,128]{1,0:T(8,128)(2,1)}, bf16[1024,1024]{1,0:T(8,128)(2,1)}) custom-call(bf16[8,160,128]{2,1,0:T(8,128)(2,1)} %get-tuple-element.25.state_ref, f32[160,128]{1,0:T(8,128)} %get-tuple-element.26.sum_ref, bf16[1024,128]{1,0:T(8,128)(2,1)} %q_ref.3, bf16[1024,128]{1,0:T(8,128)(2,1)} %k_ref.1, ...), custom_call_target="tpu_custom_call" | custom-call | tf_op jit(solution)/shard_map/pallas_call | solution.py:507
  104.3 0.0 copy-start
  104.3 0.9 slice.24
  105.2 2.8 %collective-permute-start.1 = (bf16[2,1024]{1,0:T(2,128)(2,1)S(1)}, bf16[2,1024]{1,0:T(2,128)(2,1)S(1)}, u32[]{:S(2)}, u32[]{:S(2)}) collective-permute-start(bf16[2,1024]{1,0:T(2,128)(2,1)S(1)} %slice.24), channel_id=1, source_target_pairs={{4,0},{8,4},{12,8},{16,12},{20,16},{24,20},{28,24},{5,1},{9,5},{13... | collective-permute-start | bytes 12296 | tf_op jit(solution)/shard_map/ppermute | solution.py:412
  108.0 1.8 %constant_dynamic-update-slice_fusion.1 = bf16[1026,1024]{1,0:T(8,128)(2,1)S(1)} fusion(bf16[1024,1024]{1,0:T(8,128)(2,1)} %get-tuple-element.31), kind=kLoop, calls=%fused_computation.2 | loop fusion | bytes 4194304
  109.7 0.3 collective-permute-done.1
  110.1 0.0 copy-done
  110.1 0.0 copy-start.2
  110.1 0.0 copy-start.1
  110.1 2.9 %add_convert_fusion = bf16[1024,1024]{1,0:T(8,128)(2,1)} fusion(bf16[1024,1024]{1,0:T(8,128)(2,1)S(1)} %copy-done, bf16[1026,1024]{1,0:T(8,128)(2,1)S(1)} %constant_dynamic-update-slice_fusion, f32[1024]{0:T(1024)S(1)} %bitcast.16, f32[1024]{0:T(1024)S(1)} %bitcast.17, f32[1024]{0:T(1024)S(1)} %bitcast.15), kind=kLoop, calls=%fused_computation | loop fusion | flops 9437184 | bytes 8400896 | tf_op jit(solution)/shard_map/convert_element_type | solution.py:543
  113.0 0.0 copy-done.2
  113.0 0.7 copy.15
  113.8 0.0 copy-done.1
  113.8 0.7 copy.16
  (1 shorter events, 0.0 us)
Async XLA Ops:
  1.4 8.9 %collective-permute-start = (bf16[2,1024]{1,0:T(2,128)(2,1)S(1)}, bf16[2,1024]{1,0:T(2,128)(2,1)S(1)}, u32[]{:S(2)}, u32[]{:S(2)}) collective-permute-start(bf16[2,1024]{1,0:T(2,128)(2,1)S(1)} %slice.21), channel_id=1, source_target_pairs={{0,4},{4,8},{8,12},{12,16},{16,20},{20,24},{24,28},{1,5},{5,9},{9,... | collective-permute-start | bytes 12296 | tf_op jit(solution)/shard_map/ppermute | solution.py:412
  104.3 5.8 %copy-start = (bf16[1024,1024]{1,0:T(8,128)(2,1)S(1)}, bf16[1024,1024]{1,0:T(8,128)(2,1)}, u32[]{:S(2)}) copy-start(bf16[1024,1024]{1,0:T(8,128)(2,1)} %get-tuple-element.31) | copy-start | bytes 6291460
  105.2 4.9 %collective-permute-start.1 = (bf16[2,1024]{1,0:T(2,128)(2,1)S(1)}, bf16[2,1024]{1,0:T(2,128)(2,1)S(1)}, u32[]{:S(2)}, u32[]{:S(2)}) collective-permute-start(bf16[2,1024]{1,0:T(2,128)(2,1)S(1)} %slice.24), channel_id=1, source_target_pairs={{4,0},{8,4},{12,8},{16,12},{20,16},{24,20},{28,24},{5,1},{9,5},{13... | collective-permute-start | bytes 12296 | tf_op jit(solution)/shard_map/ppermute | solution.py:412
  110.1 2.9 %copy-start.2 = (bf16[1024,128]{1,0:T(8,128)(2,1)S(1)}, bf16[1024,128]{1,0:T(8,128)(2,1)}, u32[]{:S(2)}) copy-start(bf16[1024,128]{1,0:T(8,128)(2,1)} %get-tuple-element.40) | copy-start | bytes 786436
  110.1 3.6 %copy-start.1 = (bf16[1024,128]{1,0:T(8,128)(2,1)S(1)}, bf16[1024,128]{1,0:T(8,128)(2,1)}, u32[]{:S(2)}) copy-start(bf16[1024,128]{1,0:T(8,128)(2,1)} %get-tuple-element.41) | copy-start | bytes 786436

commit v2 on v1

--- a/solution.py
+++ b/solution.py
@@ -82,7 +82,17 @@
     sum_ref[...] = jnp.where(lanes(ROWS) == h, column, sum_ref[...])
 
 
-def state_kernel(values_ref, prev_ref, taps_ref, kt_ref, conv_ref, state_ref, sum_ref):
+def state_kernel(
+    values_ref, prev_ref, taps_ref, q_ref, k_ref, conv_ref, state_ref, sum_ref, qt_ref, kt_ref
+):
+    h = pl.program_id(0)
+
+    @pl.when(h == 0)
+    def _():
+        qt_ref[...] = q_ref[...].astype(F32).T.astype(BF)
+        kt_ref[...] = k_ref[...].astype(F32).T.astype(BF)
+
+    kt = kt_ref[pl.ds(pl.multiple_of(h * FEAT, FEAT), FEAT)]
     v = values_ref[...].astype(F32)
     row = lax.broadcasted_iota(jnp.int32, v.shape, 0)
     one = jnp.where(row == 0, prev_ref[1:2], pltpu.roll(v, 1, 0))
@@ -91,19 +101,22 @@
     )
     conv = (taps_ref[0:1] * v + taps_ref[1:2] * one + taps_ref[2:3] * two).astype(BF)
     conv_ref[...] = conv
-    total = dot(phi(kt_ref[...].astype(F32), 1.0), with_ones(conv))
+    total = dot(phi(kt.astype(F32), 1.0), with_ones(conv))
     state_ref[0] = total[:, :128].astype(BF)
-    put_sum(sum_ref, pl.program_id(0), total[:, 128:129])
+    put_sum(sum_ref, h, total[:, 128:129])
 
 
 class Exchange:
     def __init__(self, sign, blocks, state_ref, sum_ref, refs):
         self.sign, self.blocks, self.chips = sign, blocks, blocks // 2
         self.state_ref, self.sum_ref = state_ref, sum_ref
-        self.states, self.sums, self.acc, self.give, self.got = refs[:5]
-        self.send, self.recv, self.swap_send, self.swap_recv = refs[5:]
+        self.states, self.sums, self.small, self.mate, self.pair = refs[:5]
+        self.acc, self.give, self.got, self.acc_s, self.give_s, self.got_s = refs[5:11]
+        self.send, self.recv, self.near = refs[11:]
+        self.half = state_ref.shape[0] // 2
         self.me = lax.axis_index("ctx")
         self.chip, self.core = self.me // 2, self.me % 2
+        self.sibling = self.me + 1 - 2 * self.core
 
     def greet(self, peers=0):
         barrier = pltpu.get_barrier_semaphore()
@@ -118,7 +131,7 @@
 
     def copies(self, d):
         to = (self.me + 2 * d * self.sign + self.blocks) % self.blocks
-        pairs = [(self.state_ref, self.states), (self.sum_ref, self.sums)]
+        pairs = [(self.pair, self.states), (self.small, self.sums)]
         return [
             pltpu.make_async_remote_copy(
                 src_ref=src,
@@ -130,14 +143,28 @@
             for k, (src, dst) in enumerate(pairs)
         ]
 
+    def beside(self, src, dst, k):
+        return pltpu.make_async_remote_copy(
+            src_ref=src,
+            dst_ref=dst,
+            send_sem=self.near.at[2 * k],
+            recv_sem=self.near.at[2 * k + 1],
+            device_id={"ctx": self.sibling},
+        )
+
+    def first(self):
+        return self.beside(
+            self.state_ref.at[pl.ds((1 - self.core) * self.half, self.half)], self.mate, 0
+        )
+
     def swap(self):
-        return pltpu.make_async_remote_copy(
-            src_ref=self.give,
-            dst_ref=self.got,
-            send_sem=self.swap_send,
-            recv_sem=self.swap_recv,
-            device_id={"ctx": self.me + 1 - 2 * self.core},
-        )
+        return [
+            self.beside(self.give, self.got, 1),
+            self.beside(self.give_s, self.got_s, 2),
+        ]
+
+    def own(self):
+        return self.state_ref[pl.ds(self.core * self.half, self.half)].astype(F32)
 
     def reaches(self, d):
         return self.chip + d < self.chips if self.sign > 0 else self.chip >= d
@@ -146,6 +173,13 @@
         return self.chip >= d if self.sign > 0 else self.chip + d < self.chips
 
     def start(self):
+        self.first().start()
+        sums = jnp.concatenate([self.sum_ref[...], jnp.zeros((256 - ROWS, 128), F32)], axis=0)
+        self.small[...] = sums.T[:8]
+
+    def spread(self):
+        self.first().wait()
+        self.pair[...] = (self.own() + self.mate[...].astype(F32)).astype(BF)
         for d in range(1, self.chips):
 
             @pl.when(self.reaches(d))
@@ -154,29 +188,36 @@
                     copy.start()
 
     def merge(self):
-        heads = self.state_ref.shape[0]
         self.acc[...] = jnp.zeros_like(self.acc)
+        self.acc_s[...] = jnp.zeros_like(self.acc_s)
         for d in range(1, self.chips):
 
             @pl.when(self.reached(d))
             def _():
                 for copy in self.copies(d):
                     copy.wait_recv()
-                self.acc[:heads] += self.states[d - 1].astype(F32)
-                self.acc[heads] += self.sums[d - 1]
+                self.acc[...] += self.states[d - 1].astype(F32)
+                self.acc_s[...] += self.sums[d - 1]
 
         self.give[...] = self.acc[...]
-
-        @pl.when(self.core == (0 if self.sign > 0 else 1))
+        self.give_s[...] = self.acc_s[...]
+        leads = self.core == (0 if self.sign > 0 else 1)
+
+        @pl.when(leads)
         def _():
-            self.give[:heads] += self.state_ref[...].astype(F32)
-            self.give[heads] += self.sum_ref[...]
-
-        self.swap().start()
+            self.give[...] += self.own()
+            self.give_s[...] += self.small[...]
+
+        for copy in self.swap():
+            copy.start()
+
+        @pl.when(jnp.logical_not(leads))
+        def _():
+            self.acc[...] += self.mate[...].astype(F32)
 
     def finish(self, out, order):
-        heads = self.state_ref.shape[0]
-        self.swap().wait()
+        for copy in self.swap():
+            copy.wait()
         for d in range(1, self.chips):
 
             @pl.when(self.reaches(d))
@@ -184,25 +225,35 @@
                 for copy in self.copies(d):
                     copy.wait_send()
 
-        sums = self.acc[heads] + self.got[heads]
-        for h in range(heads):
-            column = jnp.sum(jnp.where(lanes(ROWS) == h, sums, 0.0), axis=1, keepdims=True)
-            out[h] = with_split(self.acc[h] + self.got[h], column, order)
+        sums = jnp.concatenate([self.acc_s[...] + self.got_s[...]] * 16, axis=0).T[:ROWS]
+        for j in range(self.half):
+            for h, part in (
+                (self.core * self.half + j, self.acc),
+                ((1 - self.core) * self.half + j, self.got),
+            ):
+                column = jnp.sum(jnp.where(lanes(ROWS) == h, sums, 0.0), axis=1, keepdims=True)
+                out[h] = with_split(part[j], column, order)
 
 
 def exchange_scratch(blocks, heads):
     slots = max(blocks // 2 - 1, 1)
-    return [
-        pltpu.VMEM((slots, heads, ROWS, 128), BF),
-        pltpu.VMEM((slots, ROWS, 128), F32),
-        pltpu.VMEM((heads + 1, ROWS, 128), F32),
-        pltpu.VMEM((heads + 1, ROWS, 128), F32),
-        pltpu.VMEM((heads + 1, ROWS, 128), F32),
-        pltpu.SemaphoreType.DMA((slots, 2)),
-        pltpu.SemaphoreType.DMA((slots, 2)),
-        pltpu.SemaphoreType.DMA,
-        pltpu.SemaphoreType.DMA,
-    ]
+    half = heads // 2
+    return (
+        [
+            pltpu.VMEM((slots, half, ROWS, 128), BF),
+            pltpu.VMEM((slots, 8, 256), F32),
+            pltpu.VMEM((8, 256), F32),
+            pltpu.VMEM((half, ROWS, 128), BF),
+            pltpu.VMEM((half, ROWS, 128), BF),
+        ]
+        + [pltpu.VMEM((half, ROWS, 128), F32)] * 3
+        + [pltpu.VMEM((8, 256), F32)] * 3
+        + [
+            pltpu.SemaphoreType.DMA((slots, 2)),
+            pltpu.SemaphoreType.DMA((slots, 2)),
+            pltpu.SemaphoreType.DMA((6,)),
+        ]
+    )
 
 
 def head_rows(ref, h):
@@ -232,6 +283,10 @@
         exchange.start()
         sums[...] = jnp.zeros_like(sums)
         den_ref[...] = jnp.zeros_like(den_ref)
+
+    @pl.when(step == 1)
+    def _():
+        exchange.spread()
 
     @pl.when(step == heads - 1)
     def _():
@@ -334,6 +389,10 @@
         exchange.greet()
         exchange.start()
         acc_k[...] = jnp.zeros_like(acc_k)
+
+    @pl.when(step == 1)
+    def _():
+        exchange.spread()
 
     @pl.when(step == heads - 1)
     def _():
@@ -440,24 +499,26 @@
 
     gain2 = gain.reshape(1, channels)
     previous = shifted(values[length - margin :], "ctx", 1).astype(F32)
-    qt, kt = queries.T, keys.T
-
-    conv, local, local_sum = call(
+
+    conv, local, local_sum, qt, kt = call(
         state_kernel,
         heads,
         [
             col,
             pl.BlockSpec((margin, 128), lambda h: (0, h)),
             pl.BlockSpec((CONV, 128), lambda h: (0, h)),
-            mine,
+            tok,
+            tok,
         ],
-        [col, state, sums],
+        [col, state, sums, feat, feat],
         [
             shape((length, channels), BF),
             shape((heads, ROWS, 128), BF),
             shape((ROWS, 128), F32),
+            shape((feats, length), BF),
+            shape((feats, length), BF),
         ],
-    )(values, previous, conv_weight, kt)
+    )(values, previous, conv_weight, queries, keys)
 
     att, den, stat, prior = call(
         functools.partial(forward_kernel, blocks, peers, heads),

time: 116 us -> 105 us (0.905)
  Pallas kernels: 93.4 us -> 85.7 us
  local copies, waits for them, and re-layouts: 9.22 us -> 5.64 us
    pallas_call x1, Pallas kernels: 36 us -> 31.7 us  [per_device(): call(functools.partial(forward_kernel, blocks, peers, heads), 2 * heads,...]
    pallas_call x1, Pallas kernels: 37.4 us -> 33.5 us  [per_device(): call(functools.partial(backward_kernel, blocks, heads), 2 * heads, [state...]
    unnamed x11 -> x9, local copies, waits for them, and re-layouts: 6.76 us -> 3.18 us
  transfers between devices with their start and end apart: 2 -> 2, of which waited for: 1 -> 0; matrix products, arithmetic and copies ran while one was open for 5% -> 3% of each run, Pallas kernels for 0% -> 0%
where the time goes in v2:
time: 105 us; the launch traced here: 104 us
  Pallas kernels  85.7 us (82%)
  starting transfers between devices  7.93 us (8%)
  local copies, waits for them, and re-layouts  5.64 us (5%)
  other arithmetic  3.52 us (3%)
    pallas_call x1, Pallas kernels, per_device(): call(functools.partial(backward_kernel, blocks, heads), 2 * heads, [state...  33.5 us
    pallas_call x1, Pallas kernels, per_device(): call(functools.partial(forward_kernel, blocks, peers, heads), 2 * heads,...  31.7 us
    pallas_call x1, Pallas kernels, per_device(): call(functools.partial(norm_kernel, width), heads, [col, pad, pad, col, v...  12.8 us
    ppermute x2, starting transfers between devices, shifted(): return lax.ppermute(block, axis, route)  7.93 us
    pallas_call x1, Pallas kernels, per_device(): call(state_kernel, heads, [col, pl.BlockSpec((margin, 128), lambda h: (0,...  7.72 us
    unnamed x9, local copies, waits for them, and re-layouts  3.18 us
    convert_element_type x1, other arithmetic, per_device(): return (normed, grad_q, grad_k, total.astype(BF))  2.92 us
  transfers between devices with their start and end apart: 2, of which 0 were waited for; matrix products, arithmetic and copies ran while one was open for 3% of the time, Pallas kernels for 0%

profile of v2, /device:TPU:1, one launch (start us, length us, event | category | flops | bytes accessed | tf_op | source)
XLA Modules:
  0.0 103.5 jit_solution(3463361540338931126)
XLA Ops:
  0.6 0.7 slice.21
  1.4 4.5 %collective-permute-start = (bf16[2,1024]{1,0:T(2,128)(2,1)S(1)}, bf16[2,1024]{1,0:T(2,128)(2,1)S(1)}, u32[]{:S(2)}, u32[]{:S(2)}) collective-permute-start(bf16[2,1024]{1,0:T(2,128)(2,1)S(1)} %slice.21), channel_id=1, source_target_pairs={{0,4},{4,8},{8,12},{12,16},{16,20},{20,24},{24,28},{1,5},{5,9},{9,... | collective-permute-start | bytes 12296 | tf_op jit(solution)/shard_map/ppermute | solution.py:471
  5.9 0.8 fusion
  6.7 0.0 collective-permute-done
  6.7 0.6 convert_element_type.15.prev_ref
  7.3 7.7 %shard_map.93 = (bf16[1024,1024]{1,0:T(8,128)(2,1)}, bf16[8,160,128]{2,1,0:T(8,128)(2,1)}, f32[160,128]{1,0:T(8,128)}, bf16[128,1024]{1,0:T(8,128)(2,1)}, bf16[128,1024]{1,0:T(8,128)(2,1)}) custom-call(bf16[1024,1024]{1,0:T(8,128)(2,1)} %values_ref.1, f32[2,1024]{1,0:T(2,128)} %convert_element_type.15.prev_ref, f32[3,1024]{1,0:T(4,128)} %taps_ref.1, ...), custom_call_target="tpu_custom_call" | custom-call | tf_op jit(solution)/shard_map/pallas_call | solution.py:503
  15.0 31.7 %shard_map.94 = (f32[1024,1024]{1,0:T(8,128)}, f32[1024,128]{1,0:T(8,128)}, f32[1024,128]{1,0:T(8,128)}, bf16[8,160,256]{2,1,0:T(8,128)(2,1)}) custom-call(bf16[8,160,128]{2,1,0:T(8,128)(2,1)} %get-tuple-element.20.state_ref, f32[160,128]{1,0:T(8,128)} %get-tuple-element.21.sum_ref, bf16[1024,128]{1,0:T(8,128)(2,1)} %q_ref.5, ...), custom_call_target="tpu_custom_call" | custom-call | tf_op jit(solution)/shard_map/pallas_call | solution.py:523
  46.8 12.8 %shard_map.95 = (bf16[1024,1024]{1,0:T(8,128)(2,1)}, bf16[1024,2048]{1,0:T(8,128)(2,1)}, bf16[8,160,128]{2,1,0:T(8,128)(2,1)}, f32[160,128]{1,0:T(8,128)}) custom-call(f32[1024,1024]{1,0:T(8,128)} %get-tuple-element.25.att_ref, f32[1024,128]{1,0:T(8,128)} %get-tuple-element.26.den_ref, f32[1024,128]{1,0:T(8,128)} %get-tuple-element.27.stat_ref, ...), custom_call_target="tpu_custom_call" | custom-call | tf_op jit(solution)/shard_map/pallas_call | solution.py:555
  59.6 33.5 %shard_map.96 = (bf16[1024,128]{1,0:T(8,128)(2,1)}, bf16[1024,128]{1,0:T(8,128)(2,1)}, bf16[1024,1024]{1,0:T(8,128)(2,1)}) custom-call(bf16[8,160,128]{2,1,0:T(8,128)(2,1)} %get-tuple-element.29.state_ref, f32[160,128]{1,0:T(8,128)} %get-tuple-element.30.sum_ref, bf16[1024,128]{1,0:T(8,128)(2,1)} %q_ref.5, bf16[1024,128]{1,0:T(8,128)(2,1)} %k_ref.3, ...), custom_call_target="tpu_custom_call" | custom-call | tf_op jit(solution)/shard_map/pallas_call | solution.py:568
  93.1 0.0 copy-start
  93.1 0.9 slice.24
  93.9 3.4 %collective-permute-start.1 = (bf16[2,1024]{1,0:T(2,128)(2,1)S(1)}, bf16[2,1024]{1,0:T(2,128)(2,1)S(1)}, u32[]{:S(2)}, u32[]{:S(2)}) collective-permute-start(bf16[2,1024]{1,0:T(2,128)(2,1)S(1)} %slice.24), channel_id=1, source_target_pairs={{4,0},{8,4},{12,8},{16,12},{20,16},{24,20},{28,24},{5,1},{9,5},{13... | collective-permute-start | bytes 12296 | tf_op jit(solution)/shard_map/ppermute | solution.py:471
  97.4 1.8 %constant_dynamic-update-slice_fusion.1 = bf16[1026,1024]{1,0:T(8,128)(2,1)S(1)} fusion(bf16[1024,1024]{1,0:T(8,128)(2,1)} %get-tuple-element.35), kind=kLoop, calls=%fused_computation.2 | loop fusion | bytes 4194304
  99.2 0.0 collective-permute-done.1
  99.2 0.0 copy-done
  99.2 0.0 copy-start.2
  99.2 0.0 copy-start.1
  99.2 2.9 %add_convert_fusion = bf16[1024,1024]{1,0:T(8,128)(2,1)} fusion(bf16[1024,1024]{1,0:T(8,128)(2,1)S(1)} %copy-done, bf16[1026,1024]{1,0:T(8,128)(2,1)S(1)} %constant_dynamic-update-slice_fusion, f32[1024]{0:T(1024)S(1)} %bitcast.7, f32[1024]{0:T(1024)S(1)} %bitcast.8, f32[1024]{0:T(1024)S(1)} %bitcast.6), kind=kLoop, calls=%fused_computation | loop fusion | flops 9437184 | bytes 8400896 | tf_op jit(solution)/shard_map/convert_element_type | solution.py:604
  102.1 0.0 copy-done.2
  102.1 0.7 copy.13
  102.8 0.0 copy-done.1
  102.8 0.7 copy.14
  (1 shorter events, 0.0 us)
Async XLA Ops:
  1.4 5.4 %collective-permute-start = (bf16[2,1024]{1,0:T(2,128)(2,1)S(1)}, bf16[2,1024]{1,0:T(2,128)(2,1)S(1)}, u32[]{:S(2)}, u32[]{:S(2)}) collective-permute-start(bf16[2,1024]{1,0:T(2,128)(2,1)S(1)} %slice.21), channel_id=1, source_target_pairs={{0,4},{4,8},{8,12},{12,16},{16,20},{20,24},{24,28},{1,5},{5,9},{9,... | collective-permute-start | bytes 12296 | tf_op jit(solution)/shard_map/ppermute | solution.py:471
  93.1 6.1 %copy-start = (bf16[1024,1024]{1,0:T(8,128)(2,1)S(1)}, bf16[1024,1024]{1,0:T(8,128)(2,1)}, u32[]{:S(2)}) copy-start(bf16[1024,1024]{1,0:T(8,128)(2,1)} %get-tuple-element.35) | copy-start | bytes 6291460
  93.9 5.2 %collective-permute-start.1 = (bf16[2,1024]{1,0:T(2,128)(2,1)S(1)}, bf16[2,1024]{1,0:T(2,128)(2,1)S(1)}, u32[]{:S(2)}, u32[]{:S(2)}) collective-permute-start(bf16[2,1024]{1,0:T(2,128)(2,1)S(1)} %slice.24), channel_id=1, source_target_pairs={{4,0},{8,4},{12,8},{16,12},{20,16},{24,20},{28,24},{5,1},{9,5},{13... | collective-permute-start | bytes 12296 | tf_op jit(solution)/shard_map/ppermute | solution.py:471
  99.2 2.9 %copy-start.2 = (bf16[1024,128]{1,0:T(8,128)(2,1)S(1)}, bf16[1024,128]{1,0:T(8,128)(2,1)}, u32[]{:S(2)}) copy-start(bf16[1024,128]{1,0:T(8,128)(2,1)} %get-tuple-element.44) | copy-start | bytes 786436
  99.2 3.6 %copy-start.1 = (bf16[1024,128]{1,0:T(8,128)(2,1)S(1)}, bf16[1024,128]{1,0:T(8,128)(2,1)}, u32[]{:S(2)}) copy-start(bf16[1024,128]{1,0:T(8,128)(2,1)} %get-tuple-element.45) | copy-start | bytes 786436

commit v3 on v2

--- a/solution.py
+++ b/solution.py
@@ -11,6 +11,7 @@
 FEAT = 16
 CONV = 3
 ROWS = 160
+EDGE = 16
 TILE = 256
 S = 0.25 / math.sqrt(2.0)
 EPS = 1e-06
@@ -83,21 +84,57 @@
 
 
 def state_kernel(
-    values_ref, prev_ref, taps_ref, q_ref, k_ref, conv_ref, state_ref, sum_ref, qt_ref, kt_ref
+    blocks, values_all, values_ref, taps_ref, q_ref, k_ref,
+    conv_ref, state_ref, sum_ref, qt_ref, kt_ref, halo, send, recv,
 ):
     h = pl.program_id(0)
+    me = lax.axis_index("ctx")
+    copy = pltpu.make_async_remote_copy(
+        src_ref=values_all.at[pl.ds(values_ref.shape[0] - EDGE, EDGE)],
+        dst_ref=halo,
+        send_sem=send,
+        recv_sem=recv,
+        device_id={"ctx": (me + 1) % blocks},
+    )
 
     @pl.when(h == 0)
     def _():
+        barrier = pltpu.get_barrier_semaphore()
+
+        @pl.when(me > 0)
+        def _():
+            pl.semaphore_signal(
+                barrier, inc=1, device_id={"ctx": (me + blocks - 1) % blocks}
+            )
+
+        @pl.when(me + 1 < blocks)
+        def _():
+            pl.semaphore_wait(barrier, 1)
+            copy.start()
+
         qt_ref[...] = q_ref[...].astype(F32).T.astype(BF)
         kt_ref[...] = k_ref[...].astype(F32).T.astype(BF)
+
+        @pl.when(me > 0)
+        def _():
+            copy.wait_recv()
+
+        @pl.when(me == 0)
+        def _():
+            halo[...] = jnp.zeros_like(halo)
+
+        @pl.when(me + 1 < blocks)
+        def _():
+            copy.wait_send()
+
+    prev = halo[:, pl.ds(pl.multiple_of(h * 128, 128), 128)].astype(F32)
 
     kt = kt_ref[pl.ds(pl.multiple_of(h * FEAT, FEAT), FEAT)]
     v = values_ref[...].astype(F32)
     row = lax.broadcasted_iota(jnp.int32, v.shape, 0)
-    one = jnp.where(row == 0, prev_ref[1:2], pltpu.roll(v, 1, 0))
+    one = jnp.where(row == 0, prev[EDGE - 1 :], pltpu.roll(v, 1, 0))
     two = jnp.where(
-        row == 0, prev_ref[0:1], jnp.where(row == 1, prev_ref[1:2], pltpu.roll(v, 2, 0))
+        row == 0, prev[EDGE - 2 : EDGE - 1], jnp.where(row == 1, prev[EDGE - 1 :], pltpu.roll(v, 2, 0))
     )
     conv = (taps_ref[0:1] * v + taps_ref[1:2] * one + taps_ref[2:3] * two).astype(BF)
     conv_ref[...] = conv
@@ -118,7 +155,7 @@
         self.chip, self.core = self.me // 2, self.me % 2
         self.sibling = self.me + 1 - 2 * self.core
 
-    def greet(self, peers=0):
+    def greet(self, peers=0, edge=False):
         barrier = pltpu.get_barrier_semaphore()
         for d in range(1, self.chips):
             other = (self.me + 2 * d) % self.blocks
@@ -127,7 +164,17 @@
         for d in range(1, peers):
             other = (lax.axis_index("head") + d) % peers
             pl.semaphore_signal(barrier, inc=1, device_id={"head": other})
-        pl.semaphore_wait(barrier, self.chips + max(peers - 1, 0))
+        if edge:
+
+            @pl.when(self.me + 1 < self.blocks)
+            def _():
+                other = (self.me + 1) % self.blocks
+                pl.semaphore_signal(barrier, inc=1, device_id={"ctx": other})
+
+        number = self.chips + max(peers - 1, 0)
+        if edge:
+            number = number + jnp.where(self.me > 0, 1, 0)
+        pl.semaphore_wait(barrier, number)
 
     def copies(self, d):
         to = (self.me + 2 * d * self.sign + self.blocks) % self.blocks
@@ -373,10 +420,17 @@
     put_sum(sum_ref, h, total[:, 128:129] + total[:, 129:130])
 
 
+def back_conv(x, taps):
+    n = x.shape[0]
+    total = taps[0:1] * x + taps[1:2] * pltpu.roll(x, n - 1, 0)
+    return (total + taps[2:3] * pltpu.roll(x, n - 2, 0)).astype(BF)
+
+
 def backward_kernel(
     blocks, heads,
     state_ref, sum_ref, q_ref, k_ref, qt_ref, qth_ref, kth_ref, conv_ref, dn_ref, prior_ref,
-    gq_ref, gk_ref, dconv_ref, acc_q, acc_kt, acc_k, grad_c, later, *refs,
+    taps_ref, gq_ref, gk_ref, gv_ref, acc_q, acc_kt, acc_k, grad_c, later,
+    head, tail, after, edge_send, edge_recv, *refs,
 ):
     step = pl.program_id(0)
     h = step % heads
@@ -386,7 +440,7 @@
 
     @pl.when(step == 0)
     def _():
-        exchange.greet()
+        exchange.greet(edge=True)
         exchange.start()
         acc_k[...] = jnp.zeros_like(acc_k)
 
@@ -440,12 +494,44 @@
         kx = kth_ref[...].astype(F32)
         acc_kt[here] = phi_grad(dot_nt(later[h], with_ones(conv_ref[...])), kx)
         inter = dot_tn(phi(kx, 2.0), later[h, :, :128])
-        dconv_ref[...] = (grad_c[h] + inter).astype(BF)
+        d_conv = (grad_c[h] + inter).astype(BF)
+        cols = pl.ds(pl.multiple_of(h * 128, 128), 128)
+        head[:, cols] = d_conv[:EDGE]
+        tail[:, cols] = d_conv[length - EDGE :]
+        gv_ref[:, cols] = back_conv(d_conv.astype(F32), taps_ref[:, cols])
 
     @pl.when(step == 2 * heads - 1)
     def _():
+        me = exchange.me
+        copy = pltpu.make_async_remote_copy(
+            src_ref=head,
+            dst_ref=after,
+            send_sem=edge_send,
+            recv_sem=edge_recv,
+            device_id={"ctx": (me + blocks - 1) % blocks},
+        )
+
+        @pl.when(me > 0)
+        def _():
+            copy.start()
+
         gq_ref[...] = acc_q[...].T.astype(BF)
         gk_ref[...] = (acc_k[...] + acc_kt[...].T).astype(BF)
+
+        @pl.when(me + 1 < blocks)
+        def _():
+            copy.wait_recv()
+
+        @pl.when(me + 1 == blocks)
+        def _():
+            after[...] = jnp.zeros_like(after)
+
+        rows = jnp.concatenate([tail[...], after[...]], axis=0).astype(F32)
+        gv_ref[length - EDGE :] = back_conv(rows, taps_ref[...])[:EDGE]
+
+        @pl.when(me > 0)
+        def _():
+            copy.wait_send()
 
 
 def call(body, steps, in_specs, out_specs, out_shape, scratch=(), collective_id=None):
@@ -465,18 +551,11 @@
     )
 
 
-def shifted(block, axis, distance):
-    size = lax.axis_size(axis)
-    route = [(i - distance, i) for i in range(size) if 0 <= i - distance < size]
-    return lax.ppermute(block, axis, route)
-
-
 def per_device(width, queries, keys, values, conv_weight, gain, cotangent):
     length, channels = values.shape
     heads = queries.shape[1] // FEAT
     feats = heads * FEAT
     blocks = lax.axis_size("ctx")
-    margin = CONV - 1
     shape = jax.ShapeDtypeStruct
     peers = lax.axis_size("head")
     col = pl.BlockSpec((length, 128), lambda h: (0, h))
@@ -498,14 +577,13 @@
         return i // heads * (i % heads)
 
     gain2 = gain.reshape(1, channels)
-    previous = shifted(values[length - margin :], "ctx", 1).astype(F32)
 
     conv, local, local_sum, qt, kt = call(
-        state_kernel,
+        functools.partial(state_kernel, blocks),
         heads,
         [
+            pl.BlockSpec(memory_space=pl.ANY),
             col,
-            pl.BlockSpec((margin, 128), lambda h: (0, h)),
             pl.BlockSpec((CONV, 128), lambda h: (0, h)),
             tok,
             tok,
@@ -518,7 +596,13 @@
             shape((feats, length), BF),
             shape((feats, length), BF),
         ],
-    )(values, previous, conv_weight, queries, keys)
+        [
+            pltpu.VMEM((EDGE, channels), BF),
+            pltpu.SemaphoreType.DMA,
+            pltpu.SemaphoreType.DMA,
+        ],
+        2,
+    )(values, values, conv_weight, queries, keys)
 
     att, den, stat, prior = call(
         functools.partial(forward_kernel, blocks, peers, heads),
@@ -565,7 +649,7 @@
         ],
     )(att, den, stat, cotangent, gain2, qt)
 
-    grad_q, grad_k, d_conv = call(
+    grad_q, grad_k, grad_v = call(
         functools.partial(backward_kernel, blocks, heads),
         2 * heads,
         [
@@ -579,8 +663,9 @@
             pl.BlockSpec((length, 128), lambda i: (0, i % heads)),
             pl.BlockSpec((length, 256), lambda i: (0, early(i))),
             pl.BlockSpec((1, ROWS, 256), lambda i: (early(i), 0, 0)),
+            pl.BlockSpec((CONV, channels), lambda i: (0, 0)),
         ],
-        [tok, tok, pl.BlockSpec((length, 128), lambda i: (0, late(i)))],
+        [tok, tok, pl.BlockSpec((length, channels), lambda i: (0, 0))],
         [
             shape((length, feats), BF),
             shape((length, feats), BF),
@@ -593,15 +678,12 @@
             pltpu.VMEM((heads, length, 128), F32),
             pltpu.VMEM((heads, ROWS, 256), BF),
         ]
+        + [pltpu.VMEM((EDGE, channels), BF)] * 3
+        + [pltpu.SemaphoreType.DMA] * 2
         + exchange_scratch(blocks, heads),
         1,
-    )(back, back_sum, queries, keys, qt, qt, kt, conv, dn, prior)
-    following = shifted(d_conv[:margin], "ctx", -1)
-    extended = jnp.concatenate([d_conv, following], axis=0)
-    total = jnp.zeros(values.shape, F32)
-    for tap in range(CONV):
-        total = total + conv_weight[tap] * extended[tap : tap + length]
-    return (normed, grad_q, grad_k, total.astype(BF))
+    )(back, back_sum, queries, keys, qt, qt, kt, conv, dn, prior, conv_weight)
+    return (normed, grad_q, grad_k, grad_v)
 
 
 def solution(mesh):

time: 105 us -> 101 us (0.962)
  starting transfers between devices: 7.93 us -> 0 us
  Pallas kernels: 85.7 us -> 93.3 us
  other arithmetic: 3.52 us -> 0 us
    ppermute x2 -> x0, starting transfers between devices: 7.93 us -> none  [shifted(): return lax.ppermute(block, axis, route)]
    pallas_call x1, Pallas kernels: 7.72 us -> 11.6 us  [per_device(): call(functools.partial(state_kernel, blocks), heads, [pl.BlockSpec(memory...]
    pallas_call x1, Pallas kernels: 33.5 us -> 37.2 us  [per_device(): call(functools.partial(backward_kernel, blocks, heads), 2 * heads, [state...]
    convert_element_type x2 -> x0, other arithmetic: 3.52 us -> none  [the longest x1 2.92 us: per_device(): return (normed, grad_q, grad_k, total.astype(BF))]
    unnamed x9 -> x3, local copies, waits for them, and re-layouts: 3.18 us -> 6.42 us
    slice x3 -> x0, local copies, waits for them, and re-layouts: 2.44 us -> none  [the longest x1 0.87 us: per_device(): following = shifted(d_conv[:margin], 'ctx', -1)]
  transfers between devices with their start and end apart: 2 -> 0, of which waited for: 0 -> 0; matrix products, arithmetic and copies ran while one was open for 3% -> 0% of each run, Pallas kernels for 0% -> 0%
where the time goes in v3:
time: 101 us; the launch traced here: 100 us
  Pallas kernels  93.3 us (92%)
  local copies, waits for them, and re-layouts  6.42 us (6%)
    pallas_call x1, Pallas kernels, per_device(): call(functools.partial(backward_kernel, blocks, heads), 2 * heads, [state...  37.2 us
    pallas_call x1, Pallas kernels, per_device(): call(functools.partial(forward_kernel, blocks, peers, heads), 2 * heads,...  31.7 us
    pallas_call x1, Pallas kernels, per_device(): call(functools.partial(norm_kernel, width), heads, [col, pad, pad, col, v...  12.8 us
    pallas_call x1, Pallas kernels, per_device(): call(functools.partial(state_kernel, blocks), heads, [pl.BlockSpec(memory...  11.6 us
    unnamed x3, local copies, waits for them, and re-layouts  6.42 us

profile of v3, /device:TPU:1, one launch (start us, length us, event | category | flops | bytes accessed | tf_op | source)
XLA Modules:
  0.0 100.4 jit_solution(18073133270467887973)
XLA Ops:
  0.6 11.6 %shard_map.93 = (bf16[1024,1024]{1,0:T(8,128)(2,1)}, bf16[8,160,128]{2,1,0:T(8,128)(2,1)}, f32[160,128]{1,0:T(8,128)}, bf16[128,1024]{1,0:T(8,128)(2,1)}, bf16[128,1024]{1,0:T(8,128)(2,1)}) custom-call(bf16[1024,1024]{1,0:T(8,128)(2,1)} %values_ref.1, bf16[1024,1024]{1,0:T(8,128)(2,1)} %values_ref.1, f32[3,1024]{1,0:T(4,128)} %taps_ref.3, ...), custom_call_target="tpu_custom_call" | custom-call | tf_op jit(solution)/shard_map/pallas_call | solution.py:581
  12.2 31.7 %shard_map.94 = (f32[1024,1024]{1,0:T(8,128)}, f32[1024,128]{1,0:T(8,128)}, f32[1024,128]{1,0:T(8,128)}, bf16[8,160,256]{2,1,0:T(8,128)(2,1)}) custom-call(bf16[8,160,128]{2,1,0:T(8,128)(2,1)} %get-tuple-element.20.state_ref, f32[160,128]{1,0:T(8,128)} %get-tuple-element.21.sum_ref, bf16[1024,128]{1,0:T(8,128)(2,1)} %q_ref.5, ...), custom_call_target="tpu_custom_call" | custom-call | tf_op jit(solution)/shard_map/pallas_call | solution.py:607
  43.9 12.8 %shard_map.95 = (bf16[1024,1024]{1,0:T(8,128)(2,1)}, bf16[1024,2048]{1,0:T(8,128)(2,1)}, bf16[8,160,128]{2,1,0:T(8,128)(2,1)}, f32[160,128]{1,0:T(8,128)}) custom-call(f32[1024,1024]{1,0:T(8,128)} %get-tuple-element.25.att_ref, f32[1024,128]{1,0:T(8,128)} %get-tuple-element.26.den_ref, f32[1024,128]{1,0:T(8,128)} %get-tuple-element.27.stat_ref, ...), custom_call_target="tpu_custom_call" | custom-call | tf_op jit(solution)/shard_map/pallas_call | solution.py:639
  56.8 37.2 %shard_map.96 = (bf16[1024,128]{1,0:T(8,128)(2,1)}, bf16[1024,128]{1,0:T(8,128)(2,1)}, bf16[1024,1024]{1,0:T(8,128)(2,1)}) custom-call(bf16[8,160,128]{2,1,0:T(8,128)(2,1)} %get-tuple-element.29.state_ref, f32[160,128]{1,0:T(8,128)} %get-tuple-element.30.sum_ref, bf16[1024,128]{1,0:T(8,128)(2,1)} %q_ref.5, bf16[1024,128]{1,0:T(8,128)(2,1)} %k_ref.3, ...), custom_call_target="tpu_custom_call" | custom-call | tf_op jit(solution)/shard_map/pallas_call | solution.py:652
  94.0 1.7 %copy.13 = bf16[1024,128]{1,0:T(8,128)(2,1)} copy(bf16[1024,128]{1,0:T(8,128)(2,1)} %get-tuple-element.41) | data formatting | bytes 524288
  95.7 1.7 %copy.14 = bf16[1024,128]{1,0:T(8,128)(2,1)} copy(bf16[1024,128]{1,0:T(8,128)(2,1)} %get-tuple-element.42) | data formatting | bytes 524288
  97.3 3.1 %copy.15 = bf16[1024,1024]{1,0:T(8,128)(2,1)} copy(bf16[1024,1024]{1,0:T(8,128)(2,1)} %get-tuple-element.43) | data formatting | bytes 4194304
